TPU v7x, 32 devices: a whole 2x2x4 slice. The times are simulated.
32 devices in a mesh: seq: 16 (over z, y, x), dp: 2 (over core).
Axes of the slice: x: 2, y: 2, z: 4, core: 2. Of those that a mesh axis runs over, the one named last changes fastest.
Arguments:
- queries: bfloat16 [4, 1024, 4096], P('dp', 'seq'), may hold values from -300 to 300
- key_states: bfloat16 [4, 1024, 4096], P('dp', 'seq'), may hold values from -4.5 to 4.5
- value_states: bfloat16 [4, 1024, 4096], P('dp', 'seq'), may hold values from -6 to 6
- grad_output: bfloat16 [4, 1024, 4096], P('dp', 'seq'), may hold values from -6 to 6
- query_bias: bfloat16 [4096], P(('seq', 'dp')), may hold values from -5 to 5
Outputs:
- grad_queries: bfloat16 [4, 1024, 4096], P('dp', 'seq')
- grad_keys: bfloat16 [4, 1024, 4096], P('dp', 'seq')
- grad_values: bfloat16 [4, 1024, 4096], P('dp', 'seq')
- grad_bias: float32 [4096], P(('seq', 'dp'))
All inputs are finite; a program needn't handle non-finite values.
Results may differ from a plain program's by a relative error of at most 0.007.
Values may be sent and summed in bfloat16 or wider, within the bound.
A program may use at most 128 MiB of HBM per device.

v0:
```python
import math

import jax
import jax.numpy as jnp
from jax import lax
from jax.sharding import PartitionSpec as P

HDIM = 128
QBLOCKS = 4


masked_value = -1e30


def attend(query_full, key_rows, value_rows, grad_rows):
    item_count, seq_length, total_cols = query_full.shape
    head_count = total_cols // HDIM

    def heads_view(values):
        return values.reshape(item_count, seq_length, head_count, HDIM)

    query_heads = heads_view(query_full)
    key_heads = heads_view(key_rows)
    value_heads = heads_view(value_rows)
    grad_heads = heads_view(grad_rows)
    factor = 1.0 / math.sqrt(HDIM)
    block_rows = seq_length // QBLOCKS
    grad_keys = jnp.zeros((item_count, seq_length, head_count, HDIM), jnp.float32)
    grad_values = jnp.zeros((item_count, seq_length, head_count, HDIM), jnp.float32)
    query_parts = []
    for block_idx in range(QBLOCKS):
        row_start = block_idx * block_rows
        key_end = row_start + block_rows
        block_query = query_heads[:, row_start:key_end]
        seen_keys = key_heads[:, :key_end]
        seen_values = value_heads[:, :key_end]
        block_grad = grad_heads[:, row_start:key_end]
        scores = (
            jnp.einsum(
                "nqhd,nkhd->nhqk", block_query, seen_keys, preferred_element_type=jnp.float32
            )
            * factor
        )
        row_ids = row_start + jnp.arange(block_rows)[:, None]
        key_ids = jnp.arange(key_end)[None, :]
        scores = jnp.where(key_ids <= row_ids, scores, masked_value)
        highest = jnp.max(scores, axis=-1, keepdims=True)
        shifted = jnp.exp(scores - highest)
        weights = shifted / jnp.sum(shifted, axis=-1, keepdims=True)
        grad_probs = jnp.einsum(
            "nqhd,nkhd->nhqk", block_grad, seen_values, preferred_element_type=jnp.float32
        )
        row_dot = jnp.sum(weights * grad_probs, axis=-1, keepdims=True)
        grad_scores = (weights * (grad_probs - row_dot) * factor).astype(jnp.bfloat16)
        weights_low = weights.astype(jnp.bfloat16)
        grad_values = grad_values.at[:, :key_end].add(
            jnp.einsum(
                "nhqk,nqhd->nkhd", weights_low, block_grad, preferred_element_type=jnp.float32
            )
        )
        grad_keys = grad_keys.at[:, :key_end].add(
            jnp.einsum(
                "nhqk,nqhd->nkhd", grad_scores, block_query, preferred_element_type=jnp.float32
            )
        )
        query_parts.append(
            jnp.einsum(
                "nhqk,nkhd->nqhd", grad_scores, seen_keys, preferred_element_type=jnp.float32
            )
        )
    grad_queries = jnp.concatenate(query_parts, axis=1)
    shape_out = (item_count, seq_length, total_cols)
    return (
        grad_queries.reshape(shape_out),
        grad_keys.reshape(shape_out),
        grad_values.reshape(shape_out),
    )


def head_gradients(pieces, bias_cols):
    query_rows, key_rows, value_rows, grad_rows = pieces
    query_full = (
        query_rows.astype(jnp.float32) + bias_cols.astype(jnp.float32)[None, None, :]
    ).astype(jnp.bfloat16)
    grad_q, grad_k, grad_v = attend(query_full, key_rows, value_rows, grad_rows)
    column_sums = jnp.sum(grad_q, axis=1)
    return (
        grad_q.astype(jnp.bfloat16),
        grad_k.astype(jnp.bfloat16),
        grad_v.astype(jnp.bfloat16),
        column_sums,
    )


def body(queries, key_states, value_states, grad_output, query_bias):
    bias_cols = lax.all_gather(query_bias, "dp", axis=0, tiled=True)
    regrouped = (
        lax.all_to_all(queries, "seq", split_axis=2, concat_axis=1, tiled=True),
        lax.all_to_all(key_states, "seq", split_axis=2, concat_axis=1, tiled=True),
        lax.all_to_all(value_states, "seq", split_axis=2, concat_axis=1, tiled=True),
        lax.all_to_all(grad_output, "seq", split_axis=2, concat_axis=1, tiled=True),
    )
    grad_q, grad_k, grad_v, column_sums = head_gradients(regrouped, bias_cols)
    returned = (
        lax.all_to_all(grad_q, "seq", split_axis=1, concat_axis=2, tiled=True),
        lax.all_to_all(grad_k, "seq", split_axis=1, concat_axis=2, tiled=True),
        lax.all_to_all(grad_v, "seq", split_axis=1, concat_axis=2, tiled=True),
    )
    grad_queries, grad_keys, grad_values = returned
    bias_total = jnp.sum(column_sums, axis=0)
    grad_bias = lax.psum_scatter(bias_total, "dp", scatter_dimension=0, tiled=True)
    return (grad_queries, grad_keys, grad_values, grad_bias)


def solution(mesh):
    in_specs = (
        P("dp", "seq", None),
        P("dp", "seq", None),
        P("dp", "seq", None),
        P("dp", "seq", None),
        P(("seq", "dp")),
    )
    out_specs = (P("dp", "seq", None), P("dp", "seq", None), P("dp", "seq", None), P(("seq", "dp")))
    return jax.shard_map(body, mesh=mesh, in_specs=in_specs, out_specs=out_specs, check_vma=False)
```

profile of v0, /device:TPU:0, one launch (start us, length us, event | category | flops | bytes accessed | tf_op | source)
XLA Modules:
  0.0 323.7 jit_solution(6628066375870637603)
XLA Ops:
  0.6 5.0 %copy.91 = bf16[2,64,4096]{1,0,2:T(2,128)(2,1)S(1)} copy(bf16[2,64,4096]{2,1,0:T(8,128)(2,1)} %param.25) | data formatting | bytes 2097152 | tf_op args[0]
  7.9 8.3 %all-to-all-start = ((bf16[16,2,16384]{2,1,0:T(2,128)(2,1)}), bf16[16,2,16384]{2,1,0:T(2,128)(2,1)S(1)}, u32[]{:S(2)}, u32[]{:S(2)}) async-start(bf16[16,2,16384]{2,1,0:T(2,128)(2,1)} %reshape.364), calls=%async_computation | async-start | bytes 2097152 | tf_op jit(solution)/shard_map/all_to_all | solution.py:98
  16.3 5.0 %copy.94 = bf16[2,64,4096]{1,0,2:T(2,128)(2,1)S(1)} copy(bf16[2,64,4096]{2,1,0:T(8,128)(2,1)} %param.26) | data formatting | bytes 2097152 | tf_op args[1]
  23.6 17.1 %all-to-all-done = bf16[16,2,16384]{2,1,0:T(2,128)(2,1)S(1)} async-done(((bf16[16,2,16384]{2,1,0:T(2,128)(2,1)}), bf16[16,2,16384]{2,1,0:T(2,128)(2,1)S(1)}, u32[]{:S(2)}, u32[]{:S(2)}) %all-to-all-start) | async-done | bytes 1048608 | tf_op jit(solution)/shard_map/all_to_all | solution.py:98
  40.7 5.9 %all-to-all-start.1 = ((bf16[16,2,16384]{2,1,0:T(2,128)(2,1)}), bf16[16,2,16384]{2,1,0:T(2,128)(2,1)}, u32[]{:S(2)}, u32[]{:S(2)}) async-start(bf16[16,2,16384]{2,1,0:T(2,128)(2,1)} %reshape.362), calls=%async_computation.1 | async-start | bytes 2097152 | tf_op jit(solution)/shard_map/all_to_all | solution.py:99
  46.6 5.0 %copy.100 = bf16[2,64,4096]{1,0,2:T(2,128)(2,1)S(1)} copy(bf16[2,64,4096]{2,1,0:T(8,128)(2,1)} %param.27) | data formatting | bytes 2097152 | tf_op args[2]
  53.9 15.7 %all-to-all-done.1 = bf16[16,2,16384]{2,1,0:T(2,128)(2,1)} async-done(((bf16[16,2,16384]{2,1,0:T(2,128)(2,1)}), bf16[16,2,16384]{2,1,0:T(2,128)(2,1)}, u32[]{:S(2)}, u32[]{:S(2)}) %all-to-all-start.1) | async-done | bytes 1048608 | tf_op jit(solution)/shard_map/all_to_all | solution.py:99
  69.6 6.1 %all-to-all-start.3 = ((bf16[16,2,16384]{2,1,0:T(2,128)(2,1)}), bf16[16,2,16384]{2,1,0:T(2,128)(2,1)}, u32[]{:S(2)}, u32[]{:S(2)}) async-start(bf16[16,2,16384]{2,1,0:T(2,128)(2,1)} %reshape.360), calls=%async_computation.3 | async-start | bytes 2097152 | tf_op jit(solution)/shard_map/all_to_all | solution.py:100
  77.4 5.0 %copy.97 = bf16[2,64,4096]{1,0,2:T(2,128)(2,1)S(1)} copy(bf16[2,64,4096]{2,1,0:T(8,128)(2,1)} %param.28) | data formatting | bytes 2097152 | tf_op args[3]
  84.8 13.8 %all-to-all-done.3 = bf16[16,2,16384]{2,1,0:T(2,128)(2,1)} async-done(((bf16[16,2,16384]{2,1,0:T(2,128)(2,1)}), bf16[16,2,16384]{2,1,0:T(2,128)(2,1)}, u32[]{:S(2)}, u32[]{:S(2)}) %all-to-all-start.3) | async-done | bytes 1048608 | tf_op jit(solution)/shard_map/all_to_all | solution.py:100
  98.5 6.2 %all-to-all-start.2 = ((bf16[16,2,16384]{2,1,0:T(2,128)(2,1)}), bf16[16,2,16384]{2,1,0:T(2,128)(2,1)}, u32[]{:S(2)}, u32[]{:S(2)}) async-start(bf16[16,2,16384]{2,1,0:T(2,128)(2,1)} %reshape.358), calls=%async_computation.2 | async-start | bytes 2097152 | tf_op jit(solution)/shard_map/all_to_all | solution.py:101
  108.1 3.7 %copy.92 = f32[2,64,16,256]{3,1,2,0:T(8,128)} copy(bf16[2,64,16,256]{1,0,3,2:T(2,128)(2,1)S(1)} %bitcast.91) | data formatting | bytes 3145728 | tf_op jit(solution)/shard_map/convert_element_type | solution.py:83
  111.7 3.3 %reshape.350 = f32[2,1024,2,128]{3,2,1,0:T(2,128)} reshape(f32[2,16,64,256]{3,2,1,0:T(8,128)} %bitcast.92) | data formatting | bytes 4194304 | tf_op jit(solution)/shard_map/convert_element_type | solution.py:83
  115.1 5.0 %reshape.363 = bf16[4096,2,64]{2,1,0:T(2,128)(2,1)S(1)} reshape(bf16[16,2,16384]{2,1,0:T(2,128)(2,1)} %all-to-all-done.1) | data formatting | bytes 2097152
  123.9 5.0 %reshape.361 = bf16[4096,2,64]{2,1,0:T(2,128)(2,1)S(1)} reshape(bf16[16,2,16384]{2,1,0:T(2,128)(2,1)} %all-to-all-done.3) | data formatting | bytes 2097152
  128.9 3.5 %copy.101 = bf16[2,64,16,256]{3,1,2,0:T(8,128)(2,1)} copy(bf16[2,64,16,256]{1,0,3,2:T(2,128)(2,1)S(1)} %bitcast.85) | data formatting | bytes 2097152 | tf_op jit(solution)/shard_map/all_to_all | solution.py:100
  143.3 5.0 %reshape.359 = bf16[4096,2,64]{2,1,0:T(2,128)(2,1)S(1)} reshape(bf16[16,2,16384]{2,1,0:T(2,128)(2,1)} %all-to-all-done.2) | data formatting | bytes 2097152
  148.3 3.5 %copy.98 = bf16[2,64,16,256]{3,1,2,0:T(8,128)(2,1)} copy(bf16[2,64,16,256]{1,0,3,2:T(2,128)(2,1)S(1)} %bitcast.86) | data formatting | bytes 2097152 | tf_op jit(solution)/shard_map/all_to_all | solution.py:101
  162.3 4.6 %fusion.208 = (f32[2,2,256]{2,1,0:T(2,128)S(1)}, f32[2,2,256,1024]{3,2,1,0:T(8,128)}) fusion(pred[256,1024]{1,0:T(8,128)(4,1)} %iota_compare_fusion, bf16[2,1024,2,128]{3,1,2,0:T(8,128)(2,1)S(1)} %copy-done.6, bf16[2,1024,2,128]{3,2,1,0:T(2,128)(2,1)S(1)} %copy-done.3), kind=kOutput, calls=%fused_computation.169 | convolution fusion | flops 272630784 | bytes 5771264 | tf_op jit(solution)/shard_map/sub | solution.py:48
  171.4 6.0 %fusion.219 = (f32[2,2,256]{2,1,0:T(2,128)S(1)}, f32[2,2,256,768]{3,2,1,0:T(8,128)}) fusion(f32[2,2,256,768]{3,2,1,0:T(8,128)} %fusion.105, pred[256,768]{1,0:T(8,128)(4,1)S(1)} %copy-done.12), kind=kOutput, calls=%fused_computation.170 | output fusion | flops 4719359 | bytes 6492160 | tf_op jit(solution)/shard_map/sub | solution.py:48
  177.3 10.7 %fusion.78 = f32[2,1024,2,128]{1,3,2,0:T(8,128)} fusion(f32[2,1024,2,128]{1,3,2,0:T(8,128)} %scatter-add.20, f32[2,2,256,512]{3,2,1,0:T(8,128)} %fusion.107, bf16[2,1024,2,128]{3,1,2,0:T(8,128)(2,1)S(1)} %copy-done.6, f32[2,2,256,512]{3,2,1,0:T(8,128)} %get-tuple-element.135, f32[2,2,256]{2,1,0:T(2,128)S(1)} %get-tuple-element.134), kind=kOutput, calls=%fused_computation.68 | convolution fusion | flops 138151424 | bytes 10756096 | tf_op jit(solution)/shard_map/nhqk,nqhd->nkhd/dot_general | solution.py:62
  188.1 12.2 %fusion.49 = f32[2,1024,2,128]{1,3,2,0:T(8,128)} fusion(f32[2,1024,2,128]{1,3,2,0:T(8,128)} %fusion.78, f32[2,2,256,768]{3,2,1,0:T(8,128)} %fusion.102, bf16[2,1024,2,128]{3,1,2,0:T(8,128)(2,1)S(1)} %copy-done.6, f32[2,2,256,768]{3,2,1,0:T(8,128)} %get-tuple-element.132, f32[2,2,256]{2,1,0:T(2,128)S(1)} %get-tuple-element.131), kind=kOutput, calls=%fused_computation.49 | convolution fusion | flops 207226624 | bytes 15998976 | tf_op jit(solution)/shard_map/nhqk,nqhd->nkhd/dot_general | solution.py:62
  200.3 12.6 %fusion.23 = bf16[2,1024,2,128]{1,3,2,0:T(8,128)(2,1)S(1)} fusion(f32[2,1024,2,128]{1,3,2,0:T(8,128)} %fusion.49, f32[2,2,256,1024]{3,2,1,0:T(8,128)} %fusion.128, bf16[2,1024,2,128]{3,1,2,0:T(8,128)(2,1)S(1)} %copy-done.6, f32[2,2,256,1024]{3,2,1,0:T(8,128)} %get-tuple-element.129, f32[2,2,256]{2,1,0:T(2,128)S(1)} %get-tuple-element.128), kind=kOutput, calls=%fused_computation.25 | convolution fusion | flops 276826112 | bytes 20193280 | tf_op jit(solution)/shard_map/nhqk,nqhd->nkhd/dot_general | solution.py:62
  214.9 7.0 %all-to-all-start.5 = ((bf16[2,1024,256]{2,0,1:T(2,128)(2,1)}), bf16[2,1024,256]{2,0,1:T(2,128)(2,1)S(1)}, u32[]{:S(2)}, u32[]{:S(2)}) async-start(bf16[2,1024,256]{2,0,1:T(2,128)(2,1)} %copy.123), calls=%async_computation.5 | async-start | bytes 2097152 | tf_op jit(solution)/shard_map/all_to_all | solution.py:106
  233.3 11.2 %all-to-all-done.5 = bf16[2,1024,256]{2,0,1:T(2,128)(2,1)S(1)} async-done(((bf16[2,1024,256]{2,0,1:T(2,128)(2,1)}), bf16[2,1024,256]{2,0,1:T(2,128)(2,1)S(1)}, u32[]{:S(2)}, u32[]{:S(2)}) %all-to-all-start.5) | async-done | bytes 1048608 | tf_op jit(solution)/shard_map/all_to_all | solution.py:106
  244.5 5.8 %all-to-all-start.6 = ((bf16[2,1024,256]{2,0,1:T(2,128)(2,1)}), bf16[2,1024,256]{2,0,1:T(2,128)(2,1)S(1)}, u32[]{:S(2)}, u32[]{:S(2)}) async-start(bf16[2,1024,256]{2,0,1:T(2,128)(2,1)} %copy.131), calls=%async_computation.6 | async-start | bytes 2097152 | tf_op jit(solution)/shard_map/all_to_all | solution.py:107
  253.3 9.9 %fusion.204 = (f32[2,128]{1,0:T(2,128)S(1)}, bf16[2,256,2,128]{3,1,2,0:T(8,128)(2,1)}) fusion(bf16[2,1024,2,128]{3,1,2,0:T(8,128)(2,1)} %copy.96, f32[2,2,256,512]{3,2,1,0:T(8,128)} %fusion.107, f32[2,2,256,512]{3,2,1,0:T(8,128)} %get-tuple-element.135, f32[2,2,256]{2,1,0:T(2,128)S(1)} %get-tuple-element.134), kind=kOutput, calls=%fused_computation.165 | convolution fusion | flops 138151168 | bytes 9184256 | tf_op jit(solution)/shard_map/nhqk,nkhd->nqhd/dot_general | solution.py:67
  263.2 11.0 %fusion.206 = (f32[2,128]{1,0:T(2,128)S(1)}, bf16[2,256,2,128]{3,1,2,0:T(8,128)(2,1)}) fusion(bf16[2,1024,2,128]{3,1,2,0:T(8,128)(2,1)} %copy.96, f32[2,2,256,768]{3,2,1,0:T(8,128)} %fusion.102, f32[2,2,256,768]{3,2,1,0:T(8,128)} %get-tuple-element.132, f32[2,2,256]{2,1,0:T(2,128)S(1)} %get-tuple-element.131), kind=kOutput, calls=%fused_computation.167 | convolution fusion | flops 207095296 | bytes 13640704 | tf_op jit(solution)/shard_map/nhqk,nkhd->nqhd/dot_general | solution.py:67
  274.2 12.2 %fusion.207 = (f32[2,128]{1,0:T(2,128)S(1)}, bf16[2,256,2,128]{3,1,2,0:T(8,128)(2,1)}) fusion(bf16[2,1024,2,128]{3,2,1,0:T(2,128)(2,1)S(1)} %copy-done.3, f32[2,2,256,1024]{3,2,1,0:T(8,128)} %fusion.128, f32[2,2,256,1024]{3,2,1,0:T(8,128)} %get-tuple-element.129, f32[2,2,256]{2,1,0:T(2,128)S(1)} %get-tuple-element.128), kind=kOutput, calls=%fused_computation.168 | convolution fusion | flops 276039424 | bytes 9704448 | tf_op jit(solution)/shard_map/nhqk,nkhd->nqhd/dot_general | solution.py:67
  288.8 3.7 %copy.115 = bf16[2,1024,256]{2,0,1:T(2,128)(2,1)} copy(bf16[2,1024,256]{1,2,0:T(8,128)(2,1)} %bitcast.96) | data formatting | bytes 2097152 | tf_op jit(solution)/shard_map/convert_element_type | solution.py:88
  292.5 6.9 %all-to-all-start.4 = ((bf16[2,1024,256]{2,0,1:T(2,128)(2,1)}), bf16[2,1024,256]{2,0,1:T(2,128)(2,1)S(1)}, u32[]{:S(2)}, u32[]{:S(2)}) async-start(bf16[2,1024,256]{2,0,1:T(2,128)(2,1)} %copy.115), calls=%async_computation.4 | async-start | bytes 2097152 | tf_op jit(solution)/shard_map/all_to_all | solution.py:105
  306.2 15.8 %all-to-all-done.4 = bf16[2,1024,256]{2,0,1:T(2,128)(2,1)S(1)} async-done(((bf16[2,1024,256]{2,0,1:T(2,128)(2,1)}), bf16[2,1024,256]{2,0,1:T(2,128)(2,1)S(1)}, u32[]{:S(2)}, u32[]{:S(2)}) %all-to-all-start.4) | async-done | bytes 1048608 | tf_op jit(solution)/shard_map/all_to_all | solution.py:105
  (89 shorter events, 69.8 us)
Async XLA Ops:
  7.9 32.8 %all-to-all-start = ((bf16[16,2,16384]{2,1,0:T(2,128)(2,1)}), bf16[16,2,16384]{2,1,0:T(2,128)(2,1)S(1)}, u32[]{:S(2)}, u32[]{:S(2)}) async-start(bf16[16,2,16384]{2,1,0:T(2,128)(2,1)} %reshape.364), calls=%async_computation | async-start | bytes 2097152 | tf_op jit(solution)/shard_map/all_to_all | solution.py:98
  40.7 28.9 %all-to-all-start.1 = ((bf16[16,2,16384]{2,1,0:T(2,128)(2,1)}), bf16[16,2,16384]{2,1,0:T(2,128)(2,1)}, u32[]{:S(2)}, u32[]{:S(2)}) async-start(bf16[16,2,16384]{2,1,0:T(2,128)(2,1)} %reshape.362), calls=%async_computation.1 | async-start | bytes 2097152 | tf_op jit(solution)/shard_map/all_to_all | solution.py:99
  51.6 24.0 %copy-start.13 = (bf16[128]{0:T(256)(128)(2,1)S(1)}, bf16[128]{0:T(256)(128)(2,1)}, u32[]{:S(2)}) copy-start(bf16[128]{0:T(256)(128)(2,1)} %param.29) | copy-start | bytes 772
  69.6 28.9 %all-to-all-start.3 = ((bf16[16,2,16384]{2,1,0:T(2,128)(2,1)}), bf16[16,2,16384]{2,1,0:T(2,128)(2,1)}, u32[]{:S(2)}, u32[]{:S(2)}) async-start(bf16[16,2,16384]{2,1,0:T(2,128)(2,1)} %reshape.360), calls=%async_computation.3 | async-start | bytes 2097152 | tf_op jit(solution)/shard_map/all_to_all | solution.py:100
  98.5 44.8 %all-to-all-start.2 = ((bf16[16,2,16384]{2,1,0:T(2,128)(2,1)}), bf16[16,2,16384]{2,1,0:T(2,128)(2,1)}, u32[]{:S(2)}, u32[]{:S(2)}) async-start(bf16[16,2,16384]{2,1,0:T(2,128)(2,1)} %reshape.358), calls=%async_computation.2 | async-start | bytes 2097152 | tf_op jit(solution)/shard_map/all_to_all | solution.py:101
  121.8 1.0 copy-start.2
  132.4 2.6 copy-start
  136.2 2.7 copy-start.4
  136.2 2.7 copy-start.5
  151.8 2.4 copy-start.1
  154.2 3.1 copy-start.7
  154.2 3.1 copy-start.8
  154.2 5.4 %copy-start.10 = (bf16[2,256,2,128]{3,2,1,0:T(2,128)(2,1)}, bf16[2,256,2,128]{3,2,1,0:T(2,128)(2,1)S(1)}, u32[]{:S(2)}) copy-start(bf16[2,256,2,128]{3,2,1,0:T(2,128)(2,1)S(1)} %get-tuple-element.119) | copy-start | bytes 786436
  159.7 2.6 copy-start.3
  159.7 2.7 copy-start.6
  169.7 1.6 copy-start.12
  214.9 29.6 %all-to-all-start.5 = ((bf16[2,1024,256]{2,0,1:T(2,128)(2,1)}), bf16[2,1024,256]{2,0,1:T(2,128)(2,1)S(1)}, u32[]{:S(2)}, u32[]{:S(2)}) async-start(bf16[2,1024,256]{2,0,1:T(2,128)(2,1)} %copy.123), calls=%async_computation.5 | async-start | bytes 2097152 | tf_op jit(solution)/shard_map/all_to_all | solution.py:106
  224.5 1.5 copy-start.9
  224.5 1.8 copy-start.16
  226.4 1.9 copy-start.15
  228.2 0.9 copy-start.11
  228.2 2.3 copy-start.17
  244.5 48.0 %all-to-all-start.6 = ((bf16[2,1024,256]{2,0,1:T(2,128)(2,1)}), bf16[2,1024,256]{2,0,1:T(2,128)(2,1)S(1)}, u32[]{:S(2)}, u32[]{:S(2)}) async-start(bf16[2,1024,256]{2,0,1:T(2,128)(2,1)} %copy.131), calls=%async_computation.6 | async-start | bytes 2097152 | tf_op jit(solution)/shard_map/all_to_all | solution.py:107
  288.8 10.6 %copy-start.14 = (u32[32]{0:T(128)S(1)}, u32[32]{0:T(128)}, u32[]{:S(2)}) copy-start(u32[32]{0:T(128)} %constant.221) | copy-start | bytes 388
  292.5 29.5 %all-to-all-start.4 = ((bf16[2,1024,256]{2,0,1:T(2,128)(2,1)}), bf16[2,1024,256]{2,0,1:T(2,128)(2,1)S(1)}, u32[]{:S(2)}, u32[]{:S(2)}) async-start(bf16[2,1024,256]{2,0,1:T(2,128)(2,1)} %copy.115), calls=%async_computation.4 | async-start | bytes 2097152 | tf_op jit(solution)/shard_map/all_to_all | solution.py:105
where the time goes:
time: 329 us; the launch traced here: 324 us
  matrix products  98.8 us (30%)
  local copies, waits for them, and re-layouts  88.4 us (27%)
  waiting for transfers between devices  73.6 us (22%)
  starting transfers between devices  46.2 us (14%)
  other arithmetic  10.3 us (3%)
  blocking collectives  4.24 us (1%)
    unnamed x50, local copies, waits for them, and re-layouts  50.9 us
    dot_general x4, matrix products, attend(): jnp.einsum('nhqk,nqhd->nkhd', grad_scores, block_query, preferred_element...  38.3 us
    dot_general x4, matrix products, attend(): jnp.einsum('nhqk,nkhd->nqhd', grad_scores, seen_keys, preferred_element_t...  36 us
    all_to_all x1, waiting for transfers between devices, body(): lax.all_to_all(queries, 'seq', split_axis=2, concat_axis=1, tiled=True)  17.1 us
    all_to_all x1, waiting for transfers between devices, body(): lax.all_to_all(grad_q, 'seq', split_axis=1, concat_axis=2, tiled=True)  15.8 us
    all_to_all x1, waiting for transfers between devices, body(): lax.all_to_all(key_states, 'seq', split_axis=2, concat_axis=1, tiled=True)  15.7 us
    all_to_all x1, waiting for transfers between devices, body(): lax.all_to_all(value_states, 'seq', split_axis=2, concat_axis=1, tiled=True)  13.8 us
    all_to_all x1, waiting for transfers between devices, body(): lax.all_to_all(grad_k, 'seq', split_axis=1, concat_axis=2, tiled=True)  11.2 us
  transfers between devices with their start and end apart: 7, of which 5 were waited for; matrix products, arithmetic and copies ran while one was open for 35% of the time, Pallas kernels for 0%

commit v1 on v0

v1 whole, which is shorter than its diff:
```python
import functools
import math

import jax
import jax.numpy as jnp
from jax import lax
from jax.experimental import pallas as pl
from jax.experimental.pallas import tpu as pltpu
from jax.sharding import PartitionSpec as P

HDIM = 128
ROWS = 256
FACTOR = 1.0 / math.sqrt(HDIM)
MESH = pl.DeviceIdType.MESH


def dot(a, b, dims):
    return lax.dot_general(a, b, (dims, ((), ())), preferred_element_type=jnp.float32)


def wait_bytes(ref, sem):
    pltpu.make_async_copy(ref, ref, sem).wait()


def kernel(
    n, chunk_heads, parts,
    q_hbm, k_hbm, v_hbm, g_hbm, bias_ref,
    dq_hbm, dk_hbm, dv_hbm, sums_ref,
    q_in, g_in, k_in, v_in,
    dq_out, dk_out, dv_out,
    k_low, v_low, k_high, v_high,
    k_acc, v_acc,
    in_recv, in_send, low_recv, low_send,
    out_recv, out_send, high_recv, high_send, last_sem,
):
    m = n // 2
    me = lax.axis_index("seq")
    upper = me >= m
    lower = me < m
    g = lax.rem(me, m)
    base = me - g
    items, rows, _ = q_hbm.shape
    half = m * rows
    cols = chunk_heads * HDIM
    own = parts * cols
    chunks = items * parts

    barrier = pltpu.get_barrier_semaphore()

    def greet(i, _):
        pl.semaphore_signal(
            barrier, inc=1, device_id={"seq": lax.rem(me + i, n)}, device_id_type=MESH
        )
        return 0

    lax.fori_loop(1, n, greet, 0)
    pl.semaphore_wait(barrier, n - 1)

    def column(owner, part):
        return pl.ds(pl.multiple_of(owner * own + part * cols, 128), cols)

    def remote(src, dst, send, recv, peer):
        pltpu.make_async_remote_copy(
            src_ref=src, dst_ref=dst, send_sem=send, recv_sem=recv,
            device_id={"seq": peer}, device_id_type=MESH,
        ).start()

    sources = (q_hbm, g_hbm, k_hbm, v_hbm)
    landing = (q_in, g_in, k_in, v_in)

    def send_inputs(c, _):
        item, part = c // parts, lax.rem(c, parts)
        mine = pl.ds(pl.multiple_of(g * rows, rows), rows)
        at = pl.ds(pl.multiple_of(me * rows, rows), rows)

        def place(a):
            return landing[a].at[c, mine if a < 2 else at]

        def step(i, _):
            shift = (m - 1) - i // 2 - lax.rem(i, 2) * (m // 2)
            to = lax.rem(g + shift, m)

            @pl.when(lower)
            def _():
                for a in (2, 3):
                    remote(
                        sources[a].at[item, :, column(to, part)], landing[a].at[c, at],
                        low_send.at[c, a - 2], low_recv.at[c, a - 2], m + to,
                    )

            @pl.when(shift > 0)
            def _():
                for a in (2, 3, 0, 1):
                    remote(
                        sources[a].at[item, :, column(to, part)], place(a),
                        in_send.at[c, a], in_recv.at[c, a], base + to,
                    )
            return 0

        lax.fori_loop(0, m, step, 0)
        for a in range(4):
            pltpu.make_async_copy(
                sources[a].at[item, :, column(g, part)], place(a), in_recv.at[c, a]
            ).start()
        return 0

    lax.fori_loop(0, chunks, send_inputs, 0)
    sums_ref[...] = jnp.zeros_like(sums_ref)

    def attend(c, part, h, offset):
        lane = pl.ds(h * HDIM, HDIM)
        total = offset + half
        k = k_in[c, :total, lane]
        v = v_in[c, :total, lane]
        k_turned = k.astype(jnp.float32).T.astype(jnp.bfloat16)
        bias = bias_ref[pl.ds(part * chunk_heads + h, 1), :]
        for block in reversed(range(half // ROWS)):
            q_rows = pl.ds(block * ROWS, ROWS)
            end = offset + (block + 1) * ROWS
            q = (q_in[c, q_rows, lane].astype(jnp.float32) + bias).astype(jnp.bfloat16)
            go = g_in[c, q_rows, lane]
            s = dot(k[:end], q, ((1,), (1,))) * FACTOR
            key_ids = lax.broadcasted_iota(jnp.int32, (ROWS, ROWS), 0)
            row_ids = lax.broadcasted_iota(jnp.int32, (ROWS, ROWS), 1)
            corner = jnp.where(key_ids <= row_ids, s[end - ROWS:], -1e30)
            s = corner if end == ROWS else jnp.concatenate([s[:end - ROWS], corner], axis=0)
            e = jnp.exp(s - jnp.max(s, axis=0, keepdims=True))
            p = e * (1.0 / jnp.sum(e, axis=0, keepdims=True))
            gp = dot(v[:end], go, ((1,), (1,)))
            row_dot = jnp.sum(p * gp, axis=0, keepdims=True)
            gs = (p * (gp - row_dot) * FACTOR).astype(jnp.bfloat16)
            dv = dot(p.astype(jnp.bfloat16), go, ((1,), (0,)))
            dk = dot(gs, q, ((1,), (0,)))
            if block == half // ROWS - 1:
                v_acc[:end, :] = dv
                k_acc[:end, :] = dk
            else:
                v_acc[:end, :] += dv
                k_acc[:end, :] += dk
            dq = dot(k_turned[:, :end], gs, ((1,), (0,))).T
            dq_out[c, q_rows, lane] = dq.astype(jnp.bfloat16)
            at = pl.ds(part * chunk_heads + h, 1)
            sums_ref[at, :] += jnp.sum(dq, axis=0, keepdims=True)
        dk_out[c, :total, lane] = k_acc[:total, :].astype(jnp.bfloat16)
        dv_out[c, :total, lane] = v_acc[:total, :].astype(jnp.bfloat16)

    results = (dq_out, dk_out, dv_out)
    finals = (dq_hbm, k_low, v_low)

    def work(c, _):
        item, part = c // parts, lax.rem(c, parts)
        wait_bytes(q_in.at[c], in_recv.at[c, 0])
        wait_bytes(g_in.at[c], in_recv.at[c, 1])
        wait_bytes(k_in.at[c, :half], in_recv.at[c, 2])
        wait_bytes(v_in.at[c, :half], in_recv.at[c, 3])

        @pl.when(lower)
        def _():
            for h in range(chunk_heads):
                attend(c, part, h, 0)

        @pl.when(upper)
        def _():
            wait_bytes(k_in.at[c, :half], low_recv.at[c, 0])
            wait_bytes(v_in.at[c, :half], low_recv.at[c, 1])
            for h in range(chunk_heads):
                attend(c, part, h, half)

        def rows_of(a, to):
            start = to * rows if a == 0 else (base + to) * rows
            return results[a].at[c, pl.ds(pl.multiple_of(start, rows), rows)]

        def step(i, _):
            shift = (m - 1) - i // 2 - lax.rem(i, 2) * (m // 2)
            to = lax.rem(g + shift, m)

            @pl.when(upper)
            def _():
                for a, high in ((1, k_high), (2, v_high)):
                    remote(
                        results[a].at[c, pl.ds(pl.multiple_of(to * rows, rows), rows)],
                        high.at[item, :, column(g, part)],
                        high_send.at[c, a - 1], high_recv.at[c, a - 1], to,
                    )

            @pl.when(shift > 0)
            def _():
                for a in range(3):
                    remote(
                        rows_of(a, to), finals[a].at[item, :, column(g, part)],
                        out_send.at[c, a], out_recv.at[c, a], base + to,
                    )
            return 0

        lax.fori_loop(0, m, step, 0)
        for a in range(3):
            pltpu.make_async_copy(
                rows_of(a, g), finals[a].at[item, :, column(g, part)], out_recv.at[c, a]
            ).start()
        return 0

    lax.fori_loop(0, chunks, work, 0)

    def arrived(c, _):
        for a in range(3):
            wait_bytes(finals[a].at[0, :, pl.ds(0, m * cols)], out_recv.at[c, a])

        @pl.when(lower)
        def _():
            for a, high in ((0, k_high), (1, v_high)):
                wait_bytes(high.at[0, :, pl.ds(0, m * cols)], high_recv.at[c, a])
        return 0

    lax.fori_loop(0, chunks, arrived, 0)

    @pl.when(lower)
    def _():
        for low, high in ((k_low, k_high), (v_low, v_high)):
            def add(i, _):
                piece = pl.ds(pl.multiple_of(i * 16, 16), 16)
                for item in range(items):
                    low[item, piece, :] = (
                        low[item, piece, :].astype(jnp.float32)
                        + high[item, piece, :].astype(jnp.float32)
                    ).astype(jnp.bfloat16)
                return 0

            lax.fori_loop(0, rows // 16, add, 0)

    ends = [
        pltpu.make_async_copy(low, out, last_sem.at[i])
        for i, (low, out) in enumerate(((k_low, dk_hbm), (v_low, dv_hbm)))
    ]
    for copy in ends:
        copy.start()

    def sent(c, _):
        less = (m - 1) * rows
        for a in range(4):
            wait_bytes(q_in.at[c, pl.ds(0, less)], in_send.at[c, a])
        for a in range(3):
            wait_bytes(dq_out.at[c, pl.ds(0, less)], out_send.at[c, a])

        @pl.when(lower)
        def _():
            for a in range(2):
                wait_bytes(q_in.at[c], low_send.at[c, a])

        @pl.when(upper)
        def _():
            for a in range(2):
                wait_bytes(dq_out.at[c], high_send.at[c, a])
        return 0

    lax.fori_loop(0, chunks, sent, 0)
    for copy in ends:
        copy.wait()


def body(n, queries, key_states, value_states, grad_output, query_bias):
    items, rows, width = queries.shape
    m = n // 2
    heads = width // HDIM // m
    parts = 2
    chunk_heads = heads // parts
    cols = chunk_heads * HDIM
    half = m * rows
    chunks = items * parts
    bf16, f32 = jnp.bfloat16, jnp.float32
    own = heads * HDIM
    group = lax.rem(lax.axis_index("seq"), m)

    whole_bias = lax.all_gather(query_bias, ("seq", "dp"), axis=0, tiled=True)
    bias = lax.dynamic_slice(whole_bias, (group * own,), (own,))
    bias = bias.astype(f32).reshape(heads, HDIM)

    result = jax.ShapeDtypeStruct(queries.shape, bf16)
    dma = pltpu.SemaphoreType.DMA
    anywhere = pl.BlockSpec(memory_space=pl.ANY)
    local = pl.BlockSpec(memory_space=pltpu.VMEM)
    grad_queries, grad_keys, grad_values, sums = pl.pallas_call(
        functools.partial(kernel, n, chunk_heads, parts),
        out_shape=(result, result, result, jax.ShapeDtypeStruct((heads, HDIM), f32)),
        in_specs=[anywhere] * 4 + [local],
        out_specs=(anywhere, anywhere, anywhere, local),
        scratch_shapes=[
            pltpu.VMEM((chunks, half, cols), bf16),
            pltpu.VMEM((chunks, half, cols), bf16),
            pltpu.VMEM((chunks, 2 * half, cols), bf16),
            pltpu.VMEM((chunks, 2 * half, cols), bf16),
            pltpu.VMEM((chunks, half, cols), bf16),
            pltpu.VMEM((chunks, 2 * half, cols), bf16),
            pltpu.VMEM((chunks, 2 * half, cols), bf16),
            pltpu.VMEM(queries.shape, bf16),
            pltpu.VMEM(queries.shape, bf16),
            pltpu.VMEM(queries.shape, bf16),
            pltpu.VMEM(queries.shape, bf16),
            pltpu.VMEM((2 * half, HDIM), f32),
            pltpu.VMEM((2 * half, HDIM), f32),
            dma((chunks, 4)), dma((chunks, 4)), dma((chunks, 2)), dma((chunks, 2)),
            dma((chunks, 3)), dma((chunks, 3)), dma((chunks, 2)), dma((chunks, 2)),
            dma((2,)),
        ],
        compiler_params=pltpu.CompilerParams(
            collective_id=0, has_side_effects=True, vmem_limit_bytes=52 * 1024 * 1024
        ),
    )(queries, key_states, value_states, grad_output, bias)

    bias_total = lax.dynamic_update_slice(
        jnp.zeros((width,), f32), sums.reshape(own), (group * own,)
    )
    grad_bias = lax.psum_scatter(bias_total, ("seq", "dp"), scatter_dimension=0, tiled=True)
    return (grad_queries, grad_keys, grad_values, grad_bias)


def solution(mesh):
    in_specs = (
        P("dp", "seq", None),
        P("dp", "seq", None),
        P("dp", "seq", None),
        P("dp", "seq", None),
        P(("seq", "dp")),
    )
    out_specs = (P("dp", "seq", None), P("dp", "seq", None), P("dp", "seq", None), P(("seq", "dp")))
    return jax.shard_map(
        functools.partial(body, mesh.shape["seq"]),
        mesh=mesh, in_specs=in_specs, out_specs=out_specs, check_vma=False,
    )
```

time: 329 us -> 229 us (0.70); the launches traced: 324 us -> 229 us
  Pallas kernels: 0 us -> 137 us
  matrix products: 98.8 us -> 0 us
  local copies, waits for them, and re-layouts: 88.4 us -> 5.53 us
  blocking collectives: 4.24 us -> 85.3 us
  waiting for transfers between devices: 73.6 us -> 0 us
  starting transfers between devices: 46.2 us -> 0 us
  other arithmetic: 10.3 us -> 0.13 us
    pallas_call x0 -> x1, Pallas kernels: none -> 137 us  [body(): pl.pallas_call(functools.partial(kernel, n, chunk_heads, parts), out_shap...]
    dot_general x17 -> x0, matrix products: 89.3 us -> none  [the longest x4 38.3 us: attend(): jnp.einsum('nhqk,nqhd->nkhd', grad_scores, block_query, preferred_element...]
    all_to_all x7 -> x0, waiting for transfers between devices: 73.6 us -> none  [the longest x1 17.1 us: body(): lax.all_to_all(queries, 'seq', split_axis=2, concat_axis=1, tiled=True)]
    all_to_all x7 -> x0, starting transfers between devices: 46.2 us -> none  [the longest x1 8.31 us: body(): lax.all_to_all(queries, 'seq', split_axis=2, concat_axis=1, tiled=True)]
    unnamed x50 -> x10, local copies, waits for them, and re-layouts: 50.9 us -> 5.41 us
    all_gather x1, blocking collectives: 1.77 us -> 43 us  [body(): whole_bias = lax.all_gather(query_bias, ('seq', 'dp'), axis=0, tiled=True)]
    unnamed x1, blocking collectives: 2.47 us -> 42.3 us
    convert_element_type x5 -> x0, local copies, waits for them, and re-layouts: 14.7 us -> none  [the longest x2 6.99 us: head_gradients(): query_rows.astype(jnp.float32)]
  transfers between devices with their start and end apart: 7 -> 0, of which waited for: 5 -> 0; matrix products, arithmetic and copies ran while one was open for 35% -> 0% of each run, Pallas kernels for 0% -> 0%
where the time goes in v1:
time: 229 us
  Pallas kernels  137 us (60%)
  blocking collectives  85.3 us (37%)
  local copies, waits for them, and re-layouts  5.53 us (2%)
    pallas_call x1, Pallas kernels, body(): pl.pallas_call(functools.partial(kernel, n, chunk_heads, parts), out_shap...  137 us
    all_gather x1, blocking collectives, body(): whole_bias = lax.all_gather(query_bias, ('seq', 'dp'), axis=0, tiled=True)  43 us
    unnamed x1, blocking collectives  42.3 us
    unnamed x10, local copies, waits for them, and re-layouts  5.41 us

profile of v1, /device:TPU:0, one launch (start us, length us, event | category | flops | bytes accessed | tf_op | source)
XLA Modules:
  0.0 228.7 jit_solution(13577331218801501186)
XLA Ops:
  0.6 0.0 copy-start.2
  0.7 0.6 copy-done.2
  1.3 43.0 %all-gather = bf16[32,1,128]{2,1,0:T(2,128)(2,1)S(1)} all-gather(bf16[1,1,128]{2,1,0:T(2,128)(2,1)S(1)} %bitcast.8), channel_id=1, replica_groups=mesh['seq'=16,'dp'=2] {'seq','dp'}, dimensions={0}, use_global_device_ids=true | all-gather | bytes 8448 | tf_op jit(solution)/shard_map/all_gather | solution.py:273
  44.3 0.1 reduce
  44.4 0.1 bitcast_convert_fusion.bias_ref
  44.4 137.1 %shard_map.84 = (bf16[2,64,4096]{2,1,0:T(8,128)(2,1)S(1)}, bf16[2,64,4096]{2,1,0:T(8,128)(2,1)}, bf16[2,64,4096]{2,1,0:T(8,128)(2,1)}, f32[4,128]{1,0:T(4,128)S(1)}) custom-call(bf16[2,64,4096]{2,1,0:T(8,128)(2,1)} %q_hbm.1, bf16[2,64,4096]{2,1,0:T(8,128)(2,1)} %k_hbm.1, bf16[2,64,4096]{2,1,0:T(8,128)(2,1)} %v_hbm.1, bf16[2,64,4096]{2,1,0:T(8,128)(2,1)} %g_hbm.1, ...), custom_call_target="tpu_custom_call" | custom-call | tf_op jit(solution)/shard_map/pallas_call | solution.py:281
  181.5 0.1 bitcast_dynamic-update-slice_fusion
  181.6 42.3 %all-reduce = f32[4096]{0:T(1024)S(1)} all-reduce(f32[4096]{0:T(1024)S(1)} %bitcast_dynamic-update-slice_fusion), channel_id=2, replica_groups=mesh['seq'=16,'dp'=2] {'seq','dp'}, use_global_device_ids=true, to_apply=%region_0.0.clone | all-reduce | flops 4096 | bytes 32768
  223.9 0.6 dynamic-slice
  224.5 0.0 copy-start.1
  224.5 1.0 copy.13
  225.5 0.6 copy-done.1
  226.1 0.0 copy-start
  226.1 1.0 copy.14
  227.1 0.6 copy-done
  227.7 1.0 copy.15
  (1 shorter events, 0.0 us)
Async XLA Ops:
  0.6 0.7 copy-start.2
  224.5 1.6 copy-start.1
  226.1 1.6 copy-start

commit v2 on v1

--- a/solution.py
+++ b/solution.py
@@ -23,15 +23,16 @@
 
 
 def kernel(
-    n, chunk_heads, parts,
+    n, cores, chunk_heads, parts, exchange,
     q_hbm, k_hbm, v_hbm, g_hbm, bias_ref,
     dq_hbm, dk_hbm, dv_hbm, sums_ref,
     q_in, g_in, k_in, v_in,
     dq_out, dk_out, dv_out,
     k_low, v_low, k_high, v_high,
-    k_acc, v_acc,
+    k_acc, v_acc, bias_in, sums_acc, sums_in,
     in_recv, in_send, low_recv, low_send,
     out_recv, out_send, high_recv, high_send, last_sem,
+    bias_recv, bias_send, sums_recv, sums_send,
 ):
     m = n // 2
     me = lax.axis_index("seq")
@@ -45,16 +46,57 @@
     own = parts * cols
     chunks = items * parts
 
+    heads = parts * chunk_heads
+    core = lax.axis_index("dp")
+    flat = me * cores + core
+
     barrier = pltpu.get_barrier_semaphore()
 
     def greet(i, _):
-        pl.semaphore_signal(
-            barrier, inc=1, device_id={"seq": lax.rem(me + i, n)}, device_id_type=MESH
+        if exchange:
+            other = lax.rem(flat + i, n * cores)
+            target = {"seq": other // cores, "dp": lax.rem(other, cores)}
+        else:
+            target = {"seq": lax.rem(me + i, n)}
+        pl.semaphore_signal(barrier, inc=1, device_id=target, device_id_type=MESH)
+        return 0
+
+    greeted = n * cores if exchange else n
+    lax.fori_loop(1, greeted, greet, 0)
+    pl.semaphore_wait(barrier, greeted - 1)
+
+    owned = flat // heads
+    workers = [(side * m + owned, dp) for side in range(2) for dp in range(cores)]
+    owners = [
+        ((g * heads + j) // cores, lax.rem(g * heads + j, cores)) for j in range(heads)
+    ]
+
+    def hand_out(targets, src_of, dst, recv, sends):
+        for i, (seq, dp) in enumerate(targets):
+            away = seq * cores + dp != flat
+
+            @pl.when(away)
+            def _():
+                pltpu.make_async_remote_copy(
+                    src_ref=src_of(i), dst_ref=dst, send_sem=sends.at[i], recv_sem=recv,
+                    device_id={"seq": seq, "dp": dp}, device_id_type=MESH,
+                ).start()
+
+            @pl.when(jnp.logical_not(away))
+            def _():
+                pltpu.make_async_copy(src_of(i), dst, recv).start()
+
+    def handed_out(targets, ref, sends):
+        for i, (seq, dp) in enumerate(targets):
+            @pl.when(seq * cores + dp != flat)
+            def _():
+                wait_bytes(ref.at[0], sends.at[i])
+
+    if exchange:
+        hand_out(
+            workers, lambda i: bias_ref, bias_in.at[lax.rem(flat, heads)],
+            bias_recv.at[0], bias_send,
         )
-        return 0
-
-    lax.fori_loop(1, n, greet, 0)
-    pl.semaphore_wait(barrier, n - 1)
 
     def column(owner, part):
         return pl.ds(pl.multiple_of(owner * own + part * cols, 128), cols)
@@ -105,7 +147,9 @@
         return 0
 
     lax.fori_loop(0, chunks, send_inputs, 0)
-    sums_ref[...] = jnp.zeros_like(sums_ref)
+    sums_acc[...] = jnp.zeros_like(sums_acc)
+    if exchange:
+        wait_bytes(bias_in, bias_recv.at[0])
 
     def attend(c, part, h, offset):
         lane = pl.ds(h * HDIM, HDIM)
@@ -113,7 +157,8 @@
         k = k_in[c, :total, lane]
         v = v_in[c, :total, lane]
         k_turned = k.astype(jnp.float32).T.astype(jnp.bfloat16)
-        bias = bias_ref[pl.ds(part * chunk_heads + h, 1), :]
+        head = part * chunk_heads + h
+        bias = bias_in[head, :1, :] if exchange else bias_ref[head, :1, :]
         for block in reversed(range(half // ROWS)):
             q_rows = pl.ds(block * ROWS, ROWS)
             end = offset + (block + 1) * ROWS
@@ -139,8 +184,7 @@
                 k_acc[:end, :] += dk
             dq = dot(k_turned[:, :end], gs, ((1,), (0,))).T
             dq_out[c, q_rows, lane] = dq.astype(jnp.bfloat16)
-            at = pl.ds(part * chunk_heads + h, 1)
-            sums_ref[at, :] += jnp.sum(dq, axis=0, keepdims=True)
+            sums_acc[head] += jnp.sum(dq.reshape(ROWS // 8, 8, HDIM), axis=0)
         dk_out[c, :total, lane] = k_acc[:total, :].astype(jnp.bfloat16)
         dv_out[c, :total, lane] = v_acc[:total, :].astype(jnp.bfloat16)
 
@@ -200,6 +244,12 @@
         return 0
 
     lax.fori_loop(0, chunks, work, 0)
+
+    if exchange:
+        hand_out(
+            owners, lambda j: sums_acc.at[j], sums_in.at[(me // m) * cores + core],
+            sums_recv.at[0], sums_send,
+        )
 
     def arrived(c, _):
         for a in range(3):
@@ -253,11 +303,18 @@
         return 0
 
     lax.fori_loop(0, chunks, sent, 0)
+    if exchange:
+        wait_bytes(sums_in, sums_recv.at[0])
+        sums_ref[...] = jnp.sum(jnp.sum(sums_in[...], axis=0), axis=0, keepdims=True)
+        handed_out(workers, bias_in, bias_send)
+        handed_out(owners, sums_acc, sums_send)
+    else:
+        sums_ref[...] = jnp.sum(sums_acc[...], axis=1)
     for copy in ends:
         copy.wait()
 
 
-def body(n, queries, key_states, value_states, grad_output, query_bias):
+def body(n, cores, queries, key_states, value_states, grad_output, query_bias):
     items, rows, width = queries.shape
     m = n // 2
     heads = width // HDIM // m
@@ -270,17 +327,23 @@
     own = heads * HDIM
     group = lax.rem(lax.axis_index("seq"), m)
 
-    whole_bias = lax.all_gather(query_bias, ("seq", "dp"), axis=0, tiled=True)
-    bias = lax.dynamic_slice(whole_bias, (group * own,), (own,))
-    bias = bias.astype(f32).reshape(heads, HDIM)
+    exchange = width == HDIM * n * cores
+    if exchange:
+        bias = jnp.broadcast_to(query_bias.astype(f32)[None, :], (8, HDIM))
+        sums_rows = 1
+    else:
+        whole_bias = lax.all_gather(query_bias, ("seq", "dp"), axis=0, tiled=True)
+        bias = lax.dynamic_slice(whole_bias, (group * own,), (own,))
+        bias = bias.astype(f32).reshape(heads, 1, HDIM)
+        sums_rows = heads
 
     result = jax.ShapeDtypeStruct(queries.shape, bf16)
     dma = pltpu.SemaphoreType.DMA
     anywhere = pl.BlockSpec(memory_space=pl.ANY)
     local = pl.BlockSpec(memory_space=pltpu.VMEM)
     grad_queries, grad_keys, grad_values, sums = pl.pallas_call(
-        functools.partial(kernel, n, chunk_heads, parts),
-        out_shape=(result, result, result, jax.ShapeDtypeStruct((heads, HDIM), f32)),
+        functools.partial(kernel, n, cores, chunk_heads, parts, exchange),
+        out_shape=(result, result, result, jax.ShapeDtypeStruct((sums_rows, HDIM), f32)),
         in_specs=[anywhere] * 4 + [local],
         out_specs=(anywhere, anywhere, anywhere, local),
         scratch_shapes=[
@@ -297,15 +360,20 @@
             pltpu.VMEM(queries.shape, bf16),
             pltpu.VMEM((2 * half, HDIM), f32),
             pltpu.VMEM((2 * half, HDIM), f32),
+            pltpu.VMEM((heads, 8, HDIM), f32),
+            pltpu.VMEM((heads, 8, HDIM), f32),
+            pltpu.VMEM((2 * cores, 8, HDIM), f32),
             dma((chunks, 4)), dma((chunks, 4)), dma((chunks, 2)), dma((chunks, 2)),
             dma((chunks, 3)), dma((chunks, 3)), dma((chunks, 2)), dma((chunks, 2)),
-            dma((2,)),
+            dma((2,)), dma((1,)), dma((2 * cores,)), dma((1,)), dma((heads,)),
         ],
         compiler_params=pltpu.CompilerParams(
             collective_id=0, has_side_effects=True, vmem_limit_bytes=52 * 1024 * 1024
         ),
     )(queries, key_states, value_states, grad_output, bias)
 
+    if exchange:
+        return (grad_queries, grad_keys, grad_values, sums.reshape(HDIM))
     bias_total = lax.dynamic_update_slice(
         jnp.zeros((width,), f32), sums.reshape(own), (group * own,)
     )
@@ -323,6 +391,6 @@
     )
     out_specs = (P("dp", "seq", None), P("dp", "seq", None), P("dp", "seq", None), P(("seq", "dp")))
     return jax.shard_map(
-        functools.partial(body, mesh.shape["seq"]),
+        functools.partial(body, mesh.shape["seq"], mesh.shape["dp"]),
         mesh=mesh, in_specs=in_specs, out_specs=out_specs, check_vma=False,
     )

time: 229 us -> 151 us (0.66)
  blocking collectives: 85.3 us -> 0 us
  Pallas kernels: 137 us -> 144 us
    all_gather x1 -> x0, blocking collectives: 43 us -> none  [body(): whole_bias = lax.all_gather(query_bias, ('seq', 'dp'), axis=0, tiled=True)]
    unnamed x1 -> x0, blocking collectives: 42.3 us -> none
    pallas_call x1, Pallas kernels: 137 us -> 144 us  [body(): pl.pallas_call(functools.partial(kernel, n, cores, chunk_heads, parts, ex...]
    unnamed x10 -> x8, local copies, waits for them, and re-layouts: 5.41 us -> 4.68 us
where the time goes in v2:
time: 151 us; the launch traced here: 150 us
  Pallas kernels  144 us (95%)
  local copies, waits for them, and re-layouts  5.34 us (4%)
    pallas_call x1, Pallas kernels, body(): pl.pallas_call(functools.partial(kernel, n, cores, chunk_heads, parts, ex...  144 us
    unnamed x8, local copies, waits for them, and re-layouts  4.68 us

profile of v2, /device:TPU:0, one launch (start us, length us, event | category | flops | bytes accessed | tf_op | source)
XLA Modules:
  0.0 149.8 jit_solution(1823742512896520946)
XLA Ops:
  0.6 0.7 broadcast_in_dim.2.bias_ref
  1.3 143.8 %shard_map.84 = (bf16[2,64,4096]{2,1,0:T(8,128)(2,1)S(1)}, bf16[2,64,4096]{2,1,0:T(8,128)(2,1)}, bf16[2,64,4096]{2,1,0:T(8,128)(2,1)}, f32[1,128]{1,0:T(1,128)S(1)}) custom-call(bf16[2,64,4096]{2,1,0:T(8,128)(2,1)} %q_hbm.1, bf16[2,64,4096]{2,1,0:T(8,128)(2,1)} %k_hbm.1, bf16[2,64,4096]{2,1,0:T(8,128)(2,1)} %v_hbm.1, bf16[2,64,4096]{2,1,0:T(8,128)(2,1)} %g_hbm.1, ...), custom_call_target="tpu_custom_call" | custom-call | tf_op jit(solution)/shard_map/pallas_call | solution.py:344
  145.1 0.0 copy-start.1
  145.1 1.0 copy.13
  146.1 0.6 copy-done.1
  146.7 0.0 copy-start
  146.7 1.0 copy.14
  147.7 0.6 copy-done
  148.3 1.0 copy.15
  149.3 0.5 copy.16
Async XLA Ops:
  145.1 1.6 %copy-start.1 = (bf16[2,64,4096]{2,1,0:T(8,128)(2,1)S(1)}, bf16[2,64,4096]{2,1,0:T(8,128)(2,1)}, u32[]{:S(2)}) copy-start(bf16[2,64,4096]{2,1,0:T(8,128)(2,1)} %get-tuple-element.17) | copy-start | bytes 3145732
  146.7 1.6 %copy-start = (bf16[2,64,4096]{2,1,0:T(8,128)(2,1)S(1)}, bf16[2,64,4096]{2,1,0:T(8,128)(2,1)}, u32[]{:S(2)}) copy-start(bf16[2,64,4096]{2,1,0:T(8,128)(2,1)} %get-tuple-element.18) | copy-start | bytes 3145732

commit v3 on v2

--- a/solution.py
+++ b/solution.py
@@ -318,7 +318,7 @@
     items, rows, width = queries.shape
     m = n // 2
     heads = width // HDIM // m
-    parts = 2
+    parts = min(4, heads)
     chunk_heads = heads // parts
     cols = chunk_heads * HDIM
     half = m * rows

time: 151 us -> 145 us (0.960)
  Pallas kernels: 144 us -> 139 us
    pallas_call x1, Pallas kernels: 144 us -> 139 us  [body(): pl.pallas_call(functools.partial(kernel, n, cores, chunk_heads, parts, ex...]
where the time goes in v3:
time: 145 us
  Pallas kernels  139 us (96%)
  local copies, waits for them, and re-layouts  5.34 us (4%)
    pallas_call x1, Pallas kernels, body(): pl.pallas_call(functools.partial(kernel, n, cores, chunk_heads, parts, ex...  139 us
    unnamed x8, local copies, waits for them, and re-layouts  4.68 us

profile of v3, /device:TPU:0, one launch (start us, length us, event | category | flops | bytes accessed | tf_op | source)
XLA Modules:
  0.0 144.8 jit_solution(403261111947038502)
XLA Ops:
  0.6 0.7 broadcast_in_dim.2.bias_ref
  1.3 138.8 %shard_map.84 = (bf16[2,64,4096]{2,1,0:T(8,128)(2,1)S(1)}, bf16[2,64,4096]{2,1,0:T(8,128)(2,1)}, bf16[2,64,4096]{2,1,0:T(8,128)(2,1)}, f32[1,128]{1,0:T(1,128)S(1)}) custom-call(bf16[2,64,4096]{2,1,0:T(8,128)(2,1)} %q_hbm.1, bf16[2,64,4096]{2,1,0:T(8,128)(2,1)} %k_hbm.1, bf16[2,64,4096]{2,1,0:T(8,128)(2,1)} %v_hbm.1, bf16[2,64,4096]{2,1,0:T(8,128)(2,1)} %g_hbm.1, ...), custom_call_target="tpu_custom_call" | custom-call | tf_op jit(solution)/shard_map/pallas_call | solution.py:344
  140.1 0.0 copy-start.1
  140.1 1.0 copy.13
  141.1 0.6 copy-done.1
  141.7 0.0 copy-start
  141.7 1.0 copy.14
  142.7 0.6 copy-done
  143.3 1.0 copy.15
  144.3 0.5 copy.16
Async XLA Ops:
  140.1 1.6 %copy-start.1 = (bf16[2,64,4096]{2,1,0:T(8,128)(2,1)S(1)}, bf16[2,64,4096]{2,1,0:T(8,128)(2,1)}, u32[]{:S(2)}) copy-start(bf16[2,64,4096]{2,1,0:T(8,128)(2,1)} %get-tuple-element.17) | copy-start | bytes 3145732
  141.7 1.6 %copy-start = (bf16[2,64,4096]{2,1,0:T(8,128)(2,1)S(1)}, bf16[2,64,4096]{2,1,0:T(8,128)(2,1)}, u32[]{:S(2)}) copy-start(bf16[2,64,4096]{2,1,0:T(8,128)(2,1)} %get-tuple-element.18) | copy-start | bytes 3145732

commit v4 on v3

--- a/solution.py
+++ b/solution.py
@@ -191,6 +191,39 @@
     results = (dq_out, dk_out, dv_out)
     finals = (dq_hbm, k_low, v_low)
 
+    def rows_of(a, c, to):
+        start = to * rows if a == 0 else (base + to) * rows
+        return results[a].at[c, pl.ds(pl.multiple_of(start, rows), rows)]
+
+    def send_results(c, chosen, first):
+        item, part = c // parts, lax.rem(c, parts)
+
+        def step(i, _):
+            shift = (m - 1) - i // 2 - lax.rem(i, 2) * (m // 2)
+            to = lax.rem(g + shift, m)
+            climbs = jnp.logical_and(to >= m // 2, g < m // 2)
+
+            if first:
+                @pl.when(upper)
+                def _():
+                    for a, high in ((1, k_high), (2, v_high)):
+                        remote(
+                            results[a].at[c, pl.ds(pl.multiple_of(to * rows, rows), rows)],
+                            high.at[item, :, column(g, part)],
+                            high_send.at[c, a - 1], high_recv.at[c, a - 1], to,
+                        )
+
+            @pl.when(jnp.logical_and(shift > 0, chosen(climbs)))
+            def _():
+                for a in range(3):
+                    remote(
+                        rows_of(a, c, to), finals[a].at[item, :, column(g, part)],
+                        out_send.at[c, a], out_recv.at[c, a], base + to,
+                    )
+            return 0
+
+        lax.fori_loop(0, m, step, 0)
+
     def work(c, _):
         item, part = c // parts, lax.rem(c, parts)
         wait_bytes(q_in.at[c], in_recv.at[c, 0])
@@ -210,36 +243,20 @@
             for h in range(chunk_heads):
                 attend(c, part, h, half)
 
-        def rows_of(a, to):
-            start = to * rows if a == 0 else (base + to) * rows
-            return results[a].at[c, pl.ds(pl.multiple_of(start, rows), rows)]
-
-        def step(i, _):
-            shift = (m - 1) - i // 2 - lax.rem(i, 2) * (m // 2)
-            to = lax.rem(g + shift, m)
-
-            @pl.when(upper)
-            def _():
-                for a, high in ((1, k_high), (2, v_high)):
-                    remote(
-                        results[a].at[c, pl.ds(pl.multiple_of(to * rows, rows), rows)],
-                        high.at[item, :, column(g, part)],
-                        high_send.at[c, a - 1], high_recv.at[c, a - 1], to,
-                    )
-
-            @pl.when(shift > 0)
-            def _():
-                for a in range(3):
-                    remote(
-                        rows_of(a, to), finals[a].at[item, :, column(g, part)],
-                        out_send.at[c, a], out_recv.at[c, a], base + to,
-                    )
-            return 0
-
-        lax.fori_loop(0, m, step, 0)
+        last = chunks - 1
+        send_results(c, lambda climbs: jnp.logical_or(jnp.logical_not(climbs), c == last), True)
+
+        @pl.when(c == last - 1)
+        def _():
+            def release(held, _):
+                send_results(held, lambda climbs: climbs, False)
+                return 0
+
+            lax.fori_loop(0, last, release, 0)
+
         for a in range(3):
             pltpu.make_async_copy(
-                rows_of(a, g), finals[a].at[item, :, column(g, part)], out_recv.at[c, a]
+                rows_of(a, c, g), finals[a].at[item, :, column(g, part)], out_recv.at[c, a]
             ).start()
         return 0
 
@@ -252,6 +269,7 @@
         )
 
     def arrived(c, _):
+        item, part = c // parts, lax.rem(c, parts)
         for a in range(3):
             wait_bytes(finals[a].at[0, :, pl.ds(0, m * cols)], out_recv.at[c, a])
 
@@ -259,23 +277,20 @@
         def _():
             for a, high in ((0, k_high), (1, v_high)):
                 wait_bytes(high.at[0, :, pl.ds(0, m * cols)], high_recv.at[c, a])
-        return 0
-
-    lax.fori_loop(0, chunks, arrived, 0)
-
-    @pl.when(lower)
-    def _():
-        for low, high in ((k_low, k_high), (v_low, v_high)):
-            def add(i, _):
-                piece = pl.ds(pl.multiple_of(i * 16, 16), 16)
-                for item in range(items):
-                    low[item, piece, :] = (
-                        low[item, piece, :].astype(jnp.float32)
-                        + high[item, piece, :].astype(jnp.float32)
+
+            def add(owner, _):
+                lanes = column(owner, part)
+                for low, high in ((k_low, k_high), (v_low, v_high)):
+                    low[item, :, lanes] = (
+                        low[item, :, lanes].astype(jnp.float32)
+                        + high[item, :, lanes].astype(jnp.float32)
                     ).astype(jnp.bfloat16)
                 return 0
 
-            lax.fori_loop(0, rows // 16, add, 0)
+            lax.fori_loop(0, m, add, 0)
+        return 0
+
+    lax.fori_loop(0, chunks, arrived, 0)
 
     ends = [
         pltpu.make_async_copy(low, out, last_sem.at[i])

time: 145 us -> 145 us (level)
  no operation moved by 1% of the time
where the time goes in v4:
time: 145 us; the launch traced here: 144 us
  Pallas kernels  138 us (95%)
  local copies, waits for them, and re-layouts  5.34 us (4%)
    pallas_call x1, Pallas kernels, body(): pl.pallas_call(functools.partial(kernel, n, cores, chunk_heads, parts, ex...  138 us
    unnamed x8, local copies, waits for them, and re-layouts  4.68 us

profile of v4, /device:TPU:0, one launch (start us, length us, event | category | flops | bytes accessed | tf_op | source)
XLA Modules:
  0.0 144.4 jit_solution(11311250042761495141)
XLA Ops:
  0.6 0.7 broadcast_in_dim.2.bias_ref
  1.3 138.5 %shard_map.84 = (bf16[2,64,4096]{2,1,0:T(8,128)(2,1)S(1)}, bf16[2,64,4096]{2,1,0:T(8,128)(2,1)}, bf16[2,64,4096]{2,1,0:T(8,128)(2,1)}, f32[1,128]{1,0:T(1,128)S(1)}) custom-call(bf16[2,64,4096]{2,1,0:T(8,128)(2,1)} %q_hbm.1, bf16[2,64,4096]{2,1,0:T(8,128)(2,1)} %k_hbm.1, bf16[2,64,4096]{2,1,0:T(8,128)(2,1)} %v_hbm.1, bf16[2,64,4096]{2,1,0:T(8,128)(2,1)} %g_hbm.1, ...), custom_call_target="tpu_custom_call" | custom-call | tf_op jit(solution)/shard_map/pallas_call | solution.py:359
  139.8 0.0 copy-start.1
  139.8 1.0 copy.13
  140.7 0.6 copy-done.1
  141.4 0.0 copy-start
  141.4 1.0 copy.14
  142.3 0.6 copy-done
  143.0 1.0 copy.15
  143.9 0.5 copy.16
Async XLA Ops:
  139.8 1.6 %copy-start.1 = (bf16[2,64,4096]{2,1,0:T(8,128)(2,1)S(1)}, bf16[2,64,4096]{2,1,0:T(8,128)(2,1)}, u32[]{:S(2)}) copy-start(bf16[2,64,4096]{2,1,0:T(8,128)(2,1)} %get-tuple-element.17) | copy-start | bytes 3145732
  141.4 1.6 %copy-start = (bf16[2,64,4096]{2,1,0:T(8,128)(2,1)S(1)}, bf16[2,64,4096]{2,1,0:T(8,128)(2,1)}, u32[]{:S(2)}) copy-start(bf16[2,64,4096]{2,1,0:T(8,128)(2,1)} %get-tuple-element.18) | copy-start | bytes 3145732

commit v5 on v4

--- a/solution.py
+++ b/solution.py
@@ -11,6 +11,7 @@
 HDIM = 128
 ROWS = 256
 FACTOR = 1.0 / math.sqrt(HDIM)
+AHEAD = 3
 MESH = pl.DeviceIdType.MESH
 
 
@@ -146,7 +147,7 @@
             ).start()
         return 0
 
-    lax.fori_loop(0, chunks, send_inputs, 0)
+    lax.fori_loop(0, min(AHEAD, chunks), send_inputs, 0)
     sums_acc[...] = jnp.zeros_like(sums_acc)
     if exchange:
         wait_bytes(bias_in, bias_recv.at[0])
@@ -164,12 +165,12 @@
             end = offset + (block + 1) * ROWS
             q = (q_in[c, q_rows, lane].astype(jnp.float32) + bias).astype(jnp.bfloat16)
             go = g_in[c, q_rows, lane]
-            s = dot(k[:end], q, ((1,), (1,))) * FACTOR
+            s = dot(k[:end], q, ((1,), (1,)))
             key_ids = lax.broadcasted_iota(jnp.int32, (ROWS, ROWS), 0)
             row_ids = lax.broadcasted_iota(jnp.int32, (ROWS, ROWS), 1)
             corner = jnp.where(key_ids <= row_ids, s[end - ROWS:], -1e30)
             s = corner if end == ROWS else jnp.concatenate([s[:end - ROWS], corner], axis=0)
-            e = jnp.exp(s - jnp.max(s, axis=0, keepdims=True))
+            e = jnp.exp2((s - jnp.max(s, axis=0, keepdims=True)) * (FACTOR / math.log(2.0)))
             p = e * (1.0 / jnp.sum(e, axis=0, keepdims=True))
             gp = dot(v[:end], go, ((1,), (1,)))
             row_dot = jnp.sum(p * gp, axis=0, keepdims=True)
@@ -226,6 +227,11 @@
 
     def work(c, _):
         item, part = c // parts, lax.rem(c, parts)
+
+        @pl.when(c + AHEAD < chunks)
+        def _():
+            send_inputs(c + AHEAD, 0)
+
         wait_bytes(q_in.at[c], in_recv.at[c, 0])
         wait_bytes(g_in.at[c], in_recv.at[c, 1])
         wait_bytes(k_in.at[c, :half], in_recv.at[c, 2])

time: 145 us -> 143 us (0.986)
  Pallas kernels: 138 us -> 136 us
    pallas_call x1, Pallas kernels: 138 us -> 136 us  [body(): pl.pallas_call(functools.partial(kernel, n, cores, chunk_heads, parts, ex...]
where the time goes in v5:
time: 143 us; the launch traced here: 142 us
  Pallas kernels  136 us (95%)
  local copies, waits for them, and re-layouts  5.34 us (4%)
    pallas_call x1, Pallas kernels, body(): pl.pallas_call(functools.partial(kernel, n, cores, chunk_heads, parts, ex...  136 us
    unnamed x8, local copies, waits for them, and re-layouts  4.68 us

profile of v5, /device:TPU:0, one launch (start us, length us, event | category | flops | bytes accessed | tf_op | source)
XLA Modules:
  0.0 142.5 jit_solution(13421203798854512579)
XLA Ops:
  0.6 0.7 broadcast_in_dim.2.bias_ref
  1.3 136.5 %shard_map.84 = (bf16[2,64,4096]{2,1,0:T(8,128)(2,1)S(1)}, bf16[2,64,4096]{2,1,0:T(8,128)(2,1)}, bf16[2,64,4096]{2,1,0:T(8,128)(2,1)}, f32[1,128]{1,0:T(1,128)S(1)}) custom-call(bf16[2,64,4096]{2,1,0:T(8,128)(2,1)} %q_hbm.1, bf16[2,64,4096]{2,1,0:T(8,128)(2,1)} %k_hbm.1, bf16[2,64,4096]{2,1,0:T(8,128)(2,1)} %v_hbm.1, bf16[2,64,4096]{2,1,0:T(8,128)(2,1)} %g_hbm.1, ...), custom_call_target="tpu_custom_call" | custom-call | tf_op jit(solution)/shard_map/pallas_call | solution.py:365
  137.8 0.0 copy-start.1
  137.8 1.0 copy.13
  138.7 0.6 copy-done.1
  139.4 0.0 copy-start
  139.4 1.0 copy.14
  140.3 0.6 copy-done
  141.0 1.0 copy.15
  141.9 0.5 copy.16
Async XLA Ops:
  137.8 1.6 %copy-start.1 = (bf16[2,64,4096]{2,1,0:T(8,128)(2,1)S(1)}, bf16[2,64,4096]{2,1,0:T(8,128)(2,1)}, u32[]{:S(2)}) copy-start(bf16[2,64,4096]{2,1,0:T(8,128)(2,1)} %get-tuple-element.17) | copy-start | bytes 3145732
  139.4 1.6 %copy-start = (bf16[2,64,4096]{2,1,0:T(8,128)(2,1)S(1)}, bf16[2,64,4096]{2,1,0:T(8,128)(2,1)}, u32[]{:S(2)}) copy-start(bf16[2,64,4096]{2,1,0:T(8,128)(2,1)} %get-tuple-element.18) | copy-start | bytes 3145732

commit v6 on v5

--- a/solution.py
+++ b/solution.py
@@ -196,25 +196,23 @@
         start = to * rows if a == 0 else (base + to) * rows
         return results[a].at[c, pl.ds(pl.multiple_of(start, rows), rows)]
 
-    def send_results(c, chosen, first):
+    def send_results(c):
         item, part = c // parts, lax.rem(c, parts)
 
         def step(i, _):
             shift = (m - 1) - i // 2 - lax.rem(i, 2) * (m // 2)
             to = lax.rem(g + shift, m)
-            climbs = jnp.logical_and(to >= m // 2, g < m // 2)
-
-            if first:
-                @pl.when(upper)
-                def _():
-                    for a, high in ((1, k_high), (2, v_high)):
-                        remote(
-                            results[a].at[c, pl.ds(pl.multiple_of(to * rows, rows), rows)],
-                            high.at[item, :, column(g, part)],
-                            high_send.at[c, a - 1], high_recv.at[c, a - 1], to,
-                        )
-
-            @pl.when(jnp.logical_and(shift > 0, chosen(climbs)))
+
+            @pl.when(upper)
+            def _():
+                for a, high in ((1, k_high), (2, v_high)):
+                    remote(
+                        results[a].at[c, pl.ds(pl.multiple_of(to * rows, rows), rows)],
+                        high.at[item, :, column(g, part)],
+                        high_send.at[c, a - 1], high_recv.at[c, a - 1], to,
+                    )
+
+            @pl.when(shift > 0)
             def _():
                 for a in range(3):
                     remote(
@@ -249,16 +247,7 @@
             for h in range(chunk_heads):
                 attend(c, part, h, half)
 
-        last = chunks - 1
-        send_results(c, lambda climbs: jnp.logical_or(jnp.logical_not(climbs), c == last), True)
-
-        @pl.when(c == last - 1)
-        def _():
-            def release(held, _):
-                send_results(held, lambda climbs: climbs, False)
-                return 0
-
-            lax.fori_loop(0, last, release, 0)
+        send_results(c)
 
         for a in range(3):
             pltpu.make_async_copy(

time: 143 us -> 143 us (level)
  no operation moved by 1% of the time
where the time goes in v6:
time: 143 us; the launch traced here: 142 us
  Pallas kernels  136 us (95%)
  local copies, waits for them, and re-layouts  5.34 us (4%)
    pallas_call x1, Pallas kernels, body(): pl.pallas_call(functools.partial(kernel, n, cores, chunk_heads, parts, ex...  136 us
    unnamed x8, local copies, waits for them, and re-layouts  4.68 us

profile of v6, /device:TPU:0, one launch (start us, length us, event | category | flops | bytes accessed | tf_op | source)
XLA Modules:
  0.0 142.5 jit_solution(6545732568830686772)
XLA Ops:
  0.6 0.7 broadcast_in_dim.2.bias_ref
  1.3 136.5 %shard_map.84 = (bf16[2,64,4096]{2,1,0:T(8,128)(2,1)S(1)}, bf16[2,64,4096]{2,1,0:T(8,128)(2,1)}, bf16[2,64,4096]{2,1,0:T(8,128)(2,1)}, f32[1,128]{1,0:T(1,128)S(1)}) custom-call(bf16[2,64,4096]{2,1,0:T(8,128)(2,1)} %q_hbm.1, bf16[2,64,4096]{2,1,0:T(8,128)(2,1)} %k_hbm.1, bf16[2,64,4096]{2,1,0:T(8,128)(2,1)} %v_hbm.1, bf16[2,64,4096]{2,1,0:T(8,128)(2,1)} %g_hbm.1, ...), custom_call_target="tpu_custom_call" | custom-call | tf_op jit(solution)/shard_map/pallas_call | solution.py:354
  137.8 0.0 copy-start.1
  137.8 1.0 copy.13
  138.7 0.6 copy-done.1
  139.4 0.0 copy-start
  139.4 1.0 copy.14
  140.3 0.6 copy-done
  141.0 1.0 copy.15
  141.9 0.5 copy.16
Async XLA Ops:
  137.8 1.6 %copy-start.1 = (bf16[2,64,4096]{2,1,0:T(8,128)(2,1)S(1)}, bf16[2,64,4096]{2,1,0:T(8,128)(2,1)}, u32[]{:S(2)}) copy-start(bf16[2,64,4096]{2,1,0:T(8,128)(2,1)} %get-tuple-element.17) | copy-start | bytes 3145732
  139.4 1.6 %copy-start = (bf16[2,64,4096]{2,1,0:T(8,128)(2,1)S(1)}, bf16[2,64,4096]{2,1,0:T(8,128)(2,1)}, u32[]{:S(2)}) copy-start(bf16[2,64,4096]{2,1,0:T(8,128)(2,1)} %get-tuple-element.18) | copy-start | bytes 3145732
